TPU v7x, 32 devices: a whole 2x2x4 slice. The times are simulated.
32 devices in a mesh: parts: 2 (over x), tp: 16 (over z, y, core).
Axes of the slice: x: 2, y: 2, z: 4, core: 2. Of those that a mesh axis runs over, the one named last changes fastest.
Arguments:
- tokens: bfloat16 [2048, 3072], P(('parts', 'tp')), parts along dimension 0, may hold values from -6 to 6
- routes: int32 [2048, 2], P(('parts', 'tp')), parts along dimension 0, may hold values from 0 to 7, all different within a row; in each aligned block of 64 rows (0 to 63, 64 to 127, ...) at most 18 rows name the same one
- gates: float32 [2048, 2], P(('parts', 'tp')), parts along dimension 0, may hold values from 0.25 to 1
- w_gate: bfloat16 [3072, 43008], P(None, 'tp'), may hold values from -0.109375 to 0.109375
- w_up: bfloat16 [3072, 43008], P(None, 'tp'), may hold values from -0.109375 to 0.109375
- w_down: bfloat16 [43008, 3072], P('tp'), may hold values from -0.078125 to 0.078125
Outputs:
- moe_out: bfloat16 [2048, 3072], P(('parts', 'tp')), parts along dimension 0
There are 2 independent parts, one for each index of `parts`. A program takes and returns all parts, laid end to end along the dimension named above; an argument that names none is the same for every part. Nothing has to cross between parts.
Inputs may be any that keep to these rules, and one draw needn't show every extreme that they name: `routes`: each token names 2 different experts. Within the rows of one device no expert is named more than 18 times, and in the rows of some device one expert is named exactly 18 times.
All inputs are finite; a program needn't handle non-finite values.
Results may differ from a plain program's by a relative error of at most 0.0058.
Values may be sent and summed in bfloat16 or wider, within the bound.
A program may use at most 192 MiB of HBM per device.

v0:
```python
import jax
import jax.numpy as jnp
from jax import lax
from jax.sharding import PartitionSpec as P

EXPERTS = 8
TOP = 2
CAP = 18


def swapped(x, axis, bit):
    return lax.ppermute(x, axis, [(i, i ^ 1 << bit) for i in range(lax.axis_size(axis))])


def passed_along(value, axis, steps):
    count = lax.axis_size(axis)
    pairs = [(source, (source + steps) % count) for source in range(count)]
    return lax.ppermute(value, axis, pairs)


def expert_rows(chosen_rows, w_gate, w_up, w_down):
    gate_act = jnp.dot(chosen_rows, w_gate, preferred_element_type=jnp.float32)
    up_act = jnp.dot(chosen_rows, w_up, preferred_element_type=jnp.float32)
    hidden = (jax.nn.silu(gate_act) * up_act).astype(jnp.bfloat16)
    return jnp.dot(hidden, w_down, preferred_element_type=jnp.float32)


def local(tokens, routes, gates, w_gate, w_up, w_down):
    devices = lax.axis_size("tp")
    cycle_size = devices // EXPERTS
    levels = cycle_size.bit_length() - 1
    my_index = lax.axis_index("tp")
    my_group = my_index // cycle_size
    tok_count, feat_width = tokens.shape
    routed = routes.reshape(-1)
    pair_count = routed.shape[0]
    onehot = (routed[:, None] == jnp.arange(EXPERTS, dtype=jnp.int32)[None, :]).astype(jnp.int32)
    before = jnp.cumsum(onehot, axis=0) - onehot
    slot_index = jnp.sum(before * onehot, axis=1)
    target = routed * CAP + slot_index
    source_tok = jnp.arange(pair_count, dtype=jnp.int32) // TOP
    outgoing = (
        jnp.zeros((EXPERTS * CAP, feat_width), jnp.bfloat16).at[target].set(tokens[source_tok])
    )
    outgoing = outgoing.reshape(EXPERTS, CAP, feat_width)
    group_order = (my_group - jnp.arange(EXPERTS, dtype=jnp.int32)) % EXPERTS
    spread = jnp.repeat(outgoing, cycle_size, axis=0)
    incoming = lax.all_to_all(spread, "tp", split_axis=0, concat_axis=0, tiled=True)
    flat_rows = incoming.reshape(devices * CAP, feat_width)
    partial_value = expert_rows(flat_rows, w_gate, w_up, w_down)
    partial_value = partial_value.astype(jnp.bfloat16).reshape(devices, CAP, feat_width)
    current = lax.optimization_barrier(partial_value).astype(jnp.float32)
    current = current.reshape(EXPERTS, cycle_size, CAP, feat_width)
    for bit in range(levels):
        halves = current.reshape(EXPERTS, current.shape[1] // 2, 2, CAP, feat_width)
        upper = my_index // (1 << bit) % 2 == 1
        kept = jnp.where(upper, halves[:, :, 1], halves[:, :, 0])
        sending = jnp.where(upper, halves[:, :, 0], halves[:, :, 1])
        current = kept + swapped(sending.astype(jnp.bfloat16), "tp", bit).astype(sending.dtype)
    owned = current.reshape(EXPERTS, CAP, feat_width)
    back = [lax.dynamic_index_in_dim(owned, my_group, 0, keepdims=False)]
    for offset in range(1, EXPERTS):
        chosen = lax.dynamic_index_in_dim(owned, (my_group + offset) % EXPERTS, 0, keepdims=False)
        back.append(passed_along(chosen, "tp", offset * cycle_size))
    expert_out = jnp.take(jnp.stack(back), group_order, axis=0)
    picked = expert_out.reshape(EXPERTS * CAP, feat_width)[target]
    weighted = picked.reshape(tok_count, TOP, feat_width) * gates[:, :, None]
    return jnp.sum(weighted, axis=1).astype(jnp.bfloat16)


def solution(mesh):
    in_specs = (
        P(("parts", "tp"), None),
        P(("parts", "tp"), None),
        P(("parts", "tp"), None),
        P(None, "tp"),
        P(None, "tp"),
        P("tp", None),
    )
    out_specs = P(("parts", "tp"), None)
    return jax.shard_map(local, mesh=mesh, in_specs=in_specs, out_specs=out_specs, check_vma=False)
```

profile of v0, /device:TPU:30, one launch (start us, length us, event | category | flops | bytes accessed | tf_op | source)
XLA Modules:
  0.0 188.2 jit_solution(15506965102001801274)
XLA Ops:
  2.4 4.3 %scatter_custom_fusion = bf16[144,3072]{1,0:T(8,128)(2,1)S(1)} fusion(s32[128]{0:T(128)S(1)} %get-tuple-element.16, bf16[64,3072]{1,0:T(8,128)(2,1)S(1)} %copy-done, s32[1024]{0:T(1024)S(1)} %pad_clamp_fusion.2, bf16[]{:T(256)} %constant.148.clone.1), kind=kCustom, calls=%fused_computation.19 | custom fusion | bytes 884738 | tf_op jit(solution)/shard_map/scatter | solution.py:43
  6.9 1.7 broadcast_in_dim.29
  8.6 6.0 %all-to-all-start = ((bf16[16,18,3072]{2,1,0:T(8,128)(2,1)}), bf16[16,18,3072]{2,1,0:T(8,128)(2,1)S(1)}, u32[]{:S(2)}, u32[]{:S(2)}) async-start(bf16[16,18,3072]{2,1,0:T(8,128)(2,1)} %bitcast.60), calls=%async_computation | async-start | bytes 4718592 | tf_op jit(solution)/shard_map/all_to_all | solution.py:48
  14.7 51.9 %all-to-all-done = bf16[16,18,3072]{2,1,0:T(8,128)(2,1)S(1)} async-done(((bf16[16,18,3072]{2,1,0:T(8,128)(2,1)}), bf16[16,18,3072]{2,1,0:T(8,128)(2,1)S(1)}, u32[]{:S(2)}, u32[]{:S(2)}) %all-to-all-start) | async-done | bytes 1769504 | tf_op jit(solution)/shard_map/all_to_all | solution.py:48
  66.6 1.5 reshape.213
  68.1 12.6 %fusion.21 = f32[288,2688]{1,0:T(8,128)} fusion(bf16[288,3072]{1,0:T(8,128)(2,1)} %reshape.213, bf16[3072,2688]{1,0:T(8,128)(2,1)} %param.9), kind=kOutput, calls=%fused_computation.75 | convolution fusion | flops 4756340736 | bytes 21381120 | tf_op jit(solution)/shard_map/dot_general | solution.py:22
  80.7 23.7 %fusion.2 = bf16[288,3072]{1,0:T(8,128)(2,1)} fusion(bf16[2688,3072]{1,0:T(8,128)(2,1)} %param.11, bf16[288,3072]{1,0:T(8,128)(2,1)S(1)} %copy-done.4, bf16[3072,2688]{1,0:T(8,128)(2,1)} %param.10, f32[288,2688]{1,0:T(8,128)} %fusion.21), kind=kOutput, calls=%fused_computation.7 | convolution fusion | flops 9518211072 | bytes 39665664 | tf_op jit(solution)/shard_map/dot_general | solution.py:25
  104.4 1.7 reshape.214
  106.8 1.9 %fusion.9 = bf16[8,1,18,3072]{3,0,2,1:T(8,128)(2,1)S(1)} fusion(f32[8,1,1,18,3072]{4,3,2,0,1:T(8,128)S(1)} %get-tuple-element.6, f32[8,1,1,18,3072]{4,3,2,0,1:T(8,128)S(1)} %get-tuple-element.5, pred[]{:T(512)S(6)} %eq.29), kind=kLoop, calls=%fused_computation.17 | loop fusion | flops 442368 | bytes 4423681 | tf_op jit(solution)/shard_map/convert_element_type | solution.py:59
  109.5 1.8 collective-permute-done
  111.3 4.3 %bitcast_add_fusion = f32[8,1,18,3072]{3,0,2,1:T(8,128)S(1)} fusion(bf16[8,1,18,3072]{3,0,2,1:T(8,128)(2,1)S(1)} %collective-permute-done, f32[8,1,1,18,3072]{4,3,2,0,1:T(8,128)} %copy-done.2, f32[8,1,1,18,3072]{4,3,2,0,1:T(8,128)} %copy-done.3, pred[]{:T(512)S(6)} %eq.29), kind=kLoop, calls=%fused_computation.13 | loop fusion | flops 1327104 | bytes 6193153 | tf_op jit(solution)/shard_map/add | solution.py:59
  115.6 1.8 constant_dynamic-slice_fusion
  118.4 1.6 collective-permute-start.2
  120.1 1.8 collective-permute-start.3
  123.1 1.9 %collective-permute-start.5 = (f32[18,3072]{1,0:T(8,128)S(1)}, f32[18,3072]{1,0:T(8,128)S(1)}, u32[]{:S(2)}, u32[]{:S(2)}) collective-permute-start(f32[18,3072]{1,0:T(8,128)S(1)} %bitcast.63), channel_id=1, source_target_pairs={{0,10},{1,11},{2,12},{3,13},{4,14},{5,15},{6,0},{7,1},{8,2},{9,3},... | collective-permute-start | bytes 663560 | tf_op jit(solution)/shard_map/ppermute | solution.py:18
  125.2 1.6 collective-permute-done.1
  128.9 2.5 %collective-permute-done.2 = f32[18,3072]{1,0:T(8,128)S(1)} collective-permute-done((f32[18,3072]{1,0:T(8,128)S(1)}, f32[18,3072]{1,0:T(8,128)S(1)}, u32[]{:S(2)}, u32[]{:S(2)}) %collective-permute-start.2) | collective-permute-done | bytes 221216 | tf_op jit(solution)/shard_map/ppermute | solution.py:18
  132.3 5.4 %collective-permute-done.3 = f32[18,3072]{1,0:T(8,128)S(1)} collective-permute-done((f32[18,3072]{1,0:T(8,128)S(1)}, f32[18,3072]{1,0:T(8,128)S(1)}, u32[]{:S(2)}, u32[]{:S(2)}) %collective-permute-start.3) | collective-permute-done | bytes 221216 | tf_op jit(solution)/shard_map/ppermute | solution.py:18
  138.4 33.8 %collective-permute-done.4 = f32[18,3072]{1,0:T(8,128)S(1)} collective-permute-done((f32[18,3072]{1,0:T(8,128)S(1)}, f32[18,3072]{1,0:T(8,128)S(1)}, u32[]{:S(2)}, u32[]{:S(2)}) %collective-permute-start.4) | collective-permute-done | bytes 221216 | tf_op jit(solution)/shard_map/ppermute | solution.py:18
  175.3 2.4 %gather_fusion = f32[8,18,3072]{2,1,0:T(8,128)S(1)} fusion(f32[8,18,3072]{2,1,0:T(8,128)} %bitcast_dynamic-update-slice_fusion, s32[1024]{0:T(1024)S(1)} %pad_clamp_fusion.1), kind=kCustom, calls=%fused_computation.1 | custom fusion | bytes 3538976 | tf_op jit(solution)/shard_map/jit(_take)/gather | solution.py:65
  179.1 1.7 broadcast_select_fusion
  180.8 2.3 %gather_fusion.1 = f32[128,3072]{1,0:T(8,128)} fusion(f32[144,3072]{1,0:T(8,128)S(1)} %broadcast_select_fusion, s32[1024]{0:T(1024)S(1)} %pad_clamp_fusion), kind=kCustom, calls=%fused_computation.2 | custom fusion | bytes 3146240 | tf_op jit(solution)/shard_map/gather | solution.py:66
  183.1 2.2 %reshape.215 = f32[64,2,3072]{2,1,0:T(2,128)S(1)} reshape(f32[128,3072]{1,0:T(8,128)} %gather_fusion.1) | data formatting | bytes 3145728 | tf_op jit(solution)/shard_map/reshape | solution.py:67
  185.3 2.9 %multiply_reduce_fusion = bf16[64,3072]{1,0:T(8,128)(2,1)} fusion(f32[64,2,3072]{2,1,0:T(2,128)S(1)} %reshape.215, f32[64,2]{1,0:T(8,128)S(1)} %copy.37), kind=kLoop, calls=%fused_computation.15 | loop fusion | flops 589824 | bytes 1966592 | tf_op jit(solution)/shard_map/reduce_sum | solution.py:68
  (55 shorter events, 14.5 us)
Async XLA Ops:
  0.0 2.4 %copy-start = (bf16[64,3072]{1,0:T(8,128)(2,1)S(1)}, bf16[64,3072]{1,0:T(8,128)(2,1)}, u32[]{:S(2)}) copy-start(bf16[64,3072]{1,0:T(8,128)(2,1)} %param.6) | copy-start | bytes 1179652
  8.6 57.9 %all-to-all-start = ((bf16[16,18,3072]{2,1,0:T(8,128)(2,1)}), bf16[16,18,3072]{2,1,0:T(8,128)(2,1)S(1)}, u32[]{:S(2)}, u32[]{:S(2)}) async-start(bf16[16,18,3072]{2,1,0:T(8,128)(2,1)} %bitcast.60), calls=%async_computation | async-start | bytes 4718592 | tf_op jit(solution)/shard_map/all_to_all | solution.py:48
  68.1 12.7 %copy-start.4 = (bf16[288,3072]{1,0:T(8,128)(2,1)S(1)}, bf16[288,3072]{1,0:T(8,128)(2,1)}, u32[]{:S(2)}) copy-start(bf16[288,3072]{1,0:T(8,128)(2,1)} %reshape.213) | copy-start | bytes 5308420
  106.7 1.9 %copy-start.2 = (f32[8,1,1,18,3072]{4,3,2,0,1:T(8,128)}, f32[8,1,1,18,3072]{4,3,2,0,1:T(8,128)S(1)}, u32[]{:S(2)}) copy-start(f32[8,1,1,18,3072]{4,3,2,0,1:T(8,128)S(1)} %get-tuple-element.5) | copy-start | bytes 5308420
  106.7 2.1 %copy-start.3 = (f32[8,1,1,18,3072]{4,3,2,0,1:T(8,128)}, f32[8,1,1,18,3072]{4,3,2,0,1:T(8,128)S(1)}, u32[]{:S(2)}) copy-start(f32[8,1,1,18,3072]{4,3,2,0,1:T(8,128)S(1)} %get-tuple-element.6) | copy-start | bytes 5308420
  106.7 2.6 %copy-start.5 = (f32[64,2]{0,1:T(2,128)S(1)}, f32[64,2]{0,1:T(2,128)}, u32[]{:S(2)}) copy-start(f32[64,2]{0,1:T(2,128)} %param.8) | copy-start | bytes 1540
  108.9 2.4 %collective-permute-start = (bf16[8,1,18,3072]{3,0,2,1:T(8,128)(2,1)S(1)}, bf16[8,1,18,3072]{3,0,2,1:T(8,128)(2,1)S(1)}, u32[]{:S(2)}, u32[]{:S(2)}) collective-permute-start(bf16[8,1,18,3072]{3,0,2,1:T(8,128)(2,1)S(1)} %fusion.9), channel_id=1, source_target_pairs={{0,1},{1,0},{2,3},{3,2},{4,5},{5,4},{6,7},{7,6},{8,9},{9,8},{10,11... | collective-permute-start | bytes 2654216 | tf_op jit(solution)/shard_map/ppermute | solution.py:12
  117.5 9.3 %collective-permute-start.1 = (f32[18,3072]{1,0:T(8,128)S(1)}, f32[18,3072]{1,0:T(8,128)S(1)}, u32[]{:S(2)}, u32[]{:S(2)}) collective-permute-start(f32[18,3072]{1,0:T(8,128)S(1)} %bitcast.67), channel_id=1, source_target_pairs={{0,2},{1,3},{2,4},{3,5},{4,6},{5,7},{6,8},{7,9},{8,10},{9,11},{10,... | collective-permute-start | bytes 663560 | tf_op jit(solution)/shard_map/ppermute | solution.py:18
  118.4 13.0 %collective-permute-start.2 = (f32[18,3072]{1,0:T(8,128)S(1)}, f32[18,3072]{1,0:T(8,128)S(1)}, u32[]{:S(2)}, u32[]{:S(2)}) collective-permute-start(f32[18,3072]{1,0:T(8,128)S(1)} %bitcast.66), channel_id=1, source_target_pairs={{0,4},{1,5},{2,6},{3,7},{4,8},{5,9},{6,10},{7,11},{8,12},{9,13},{1... | collective-permute-start | bytes 663560 | tf_op jit(solution)/shard_map/ppermute | solution.py:18
  120.1 17.5 %collective-permute-start.3 = (f32[18,3072]{1,0:T(8,128)S(1)}, f32[18,3072]{1,0:T(8,128)S(1)}, u32[]{:S(2)}, u32[]{:S(2)}) collective-permute-start(f32[18,3072]{1,0:T(8,128)S(1)} %bitcast.65), channel_id=1, source_target_pairs={{0,6},{1,7},{2,8},{3,9},{4,10},{5,11},{6,12},{7,13},{8,14},{9,15},... | collective-permute-start | bytes 663560 | tf_op jit(solution)/shard_map/ppermute | solution.py:18
  122.0 50.2 %collective-permute-start.4 = (f32[18,3072]{1,0:T(8,128)S(1)}, f32[18,3072]{1,0:T(8,128)S(1)}, u32[]{:S(2)}, u32[]{:S(2)}) collective-permute-start(f32[18,3072]{1,0:T(8,128)S(1)} %bitcast.64), channel_id=1, source_target_pairs={{0,8},{1,9},{2,10},{3,11},{4,12},{5,13},{6,14},{7,15},{8,0},{9,1},... | collective-permute-start | bytes 663560 | tf_op jit(solution)/shard_map/ppermute | solution.py:18
  123.1 50.0 %collective-permute-start.5 = (f32[18,3072]{1,0:T(8,128)S(1)}, f32[18,3072]{1,0:T(8,128)S(1)}, u32[]{:S(2)}, u32[]{:S(2)}) collective-permute-start(f32[18,3072]{1,0:T(8,128)S(1)} %bitcast.63), channel_id=1, source_target_pairs={{0,10},{1,11},{2,12},{3,13},{4,14},{5,15},{6,0},{7,1},{8,2},{9,3},... | collective-permute-start | bytes 663560 | tf_op jit(solution)/shard_map/ppermute | solution.py:18
  126.8 47.0 %collective-permute-start.6 = (f32[18,3072]{1,0:T(8,128)S(1)}, f32[18,3072]{1,0:T(8,128)S(1)}, u32[]{:S(2)}, u32[]{:S(2)}) collective-permute-start(f32[18,3072]{1,0:T(8,128)S(1)} %bitcast.62), channel_id=1, source_target_pairs={{0,12},{1,13},{2,14},{3,15},{4,0},{5,1},{6,2},{7,3},{8,4},{9,5},{1... | collective-permute-start | bytes 663560 | tf_op jit(solution)/shard_map/ppermute | solution.py:18
  131.4 43.2 %collective-permute-start.7 = (f32[18,3072]{1,0:T(8,128)S(1)}, f32[18,3072]{1,0:T(8,128)S(1)}, u32[]{:S(2)}, u32[]{:S(2)}) collective-permute-start(f32[18,3072]{1,0:T(8,128)S(1)} %bitcast.61), channel_id=1, source_target_pairs={{0,14},{1,15},{2,0},{3,1},{4,2},{5,3},{6,4},{7,5},{8,6},{9,7},{10,... | collective-permute-start | bytes 663560 | tf_op jit(solution)/shard_map/ppermute | solution.py:18
  180.8 7.4 %copy-start.1 = (bf16[64,3072]{1,0:T(8,128)(2,1)S(1)}, bf16[64,3072]{1,0:T(8,128)(2,1)}, u32[]{:S(2)}) copy-start(bf16[64,3072]{1,0:T(8,128)(2,1)} %param.6) | copy-start | bytes 1179652
where the time goes:
time: 189 us; the launch traced here: 188 us
  waiting for transfers between devices  97.2 us (51%)
  matrix products  36.4 us (19%)
  local copies, waits for them, and re-layouts  28.1 us (15%)
  starting transfers between devices  14.4 us (8%)
  other arithmetic  12 us (6%)
    all_to_all x1, waiting for transfers between devices, local(): lax.all_to_all(spread, 'tp', split_axis=0, concat_axis=0, tiled=True)  51.9 us
    ppermute x7, waiting for transfers between devices, passed_along(): return lax.ppermute(value, axis, pairs)  43.5 us
    dot_general x1, matrix products, expert_rows(): return jnp.dot(hidden, w_down, preferred_element_type=jnp.float32)  23.7 us
    dot_general x1, matrix products, expert_rows(): gate_act = jnp.dot(chosen_rows, w_gate, preferred_element_type=jnp.float32)  12.6 us
    ppermute x7, starting transfers between devices, passed_along(): return lax.ppermute(value, axis, pairs)  8.07 us
    unnamed x28, local copies, waits for them, and re-layouts  6.67 us
    all_to_all x1, starting transfers between devices, local(): lax.all_to_all(spread, 'tp', split_axis=0, concat_axis=0, tiled=True)  6.02 us
    add x1, other arithmetic, local(): kept + swapped(sending.astype(jnp.bfloat16), 'tp', bit).astype(sending.dt...  4.33 us
  transfers between devices with their start and end apart: 9, of which 7 were waited for; matrix products, arithmetic and copies ran while one was open for 3% of the time, Pallas kernels for 0%

commit v1 on v0

--- a/solution.py
+++ b/solution.py
@@ -1,11 +1,19 @@
+import functools
+
 import jax
 import jax.numpy as jnp
 from jax import lax
+from jax.experimental import pallas as pl
+from jax.experimental.pallas import tpu as pltpu
 from jax.sharding import PartitionSpec as P
 
 EXPERTS = 8
 TOP = 2
 CAP = 18
+BASE = 16
+MESH = pl.DeviceIdType.MESH
+BF = jnp.bfloat16
+F32 = jnp.float32
 
 
 def swapped(x, axis, bit):
@@ -25,7 +33,7 @@
     return jnp.dot(hidden, w_down, preferred_element_type=jnp.float32)
 
 
-def local(tokens, routes, gates, w_gate, w_up, w_down):
+def local_any(tokens, routes, gates, w_gate, w_up, w_down):
     devices = lax.axis_size("tp")
     cycle_size = devices // EXPERTS
     levels = cycle_size.bit_length() - 1
@@ -68,6 +76,249 @@
     return jnp.sum(weighted, axis=1).astype(jnp.bfloat16)
 
 
+PARTS = 3
+NT = 7
+
+
+def iota(shape, dim):
+    return lax.broadcasted_iota(jnp.int32, shape, dim)
+
+
+def kernel(
+    tok, routes, gates, wg, wu, wd, out,
+    w_in, w_out, acc, hid, x, send, recv_a, recv_b, own, part_s, part_r, rsend, ret, gsc,
+    in_sem, out_sem, ssem, rsem, fs_sem, fr_sem, ps_sem, pr_sem, bs_sem, br_sem,
+):
+    n_tok, feat = tok.shape
+    kc = feat // PARTS
+    ow = kc // 8
+    ff = wg.shape[1]
+    tw = ff // NT
+    rows = EXPERTS * BASE
+    ext = EXPERTS * 2
+    half = rows + ext
+    me = lax.axis_index("tp")
+    group = lax.div(me, 2)
+    core = lax.rem(me, 2)
+    twin = {"tp": group * 2 + (1 - core)}
+
+    def peer(d):
+        return lax.rem(group + d, EXPERTS)
+
+    def in_copies(c):
+        res = []
+        for j in range(NT):
+            for s, w in enumerate((wg, wu)):
+                res.append(pltpu.make_async_copy(
+                    w.at[pl.ds(c * kc, kc), pl.ds(j * tw, tw)],
+                    w_in.at[c, :, pl.ds((2 * j + s) * tw, tw)],
+                    in_sem.at[c, 2 * j + s]))
+        return res
+
+    def out_copy(n):
+        return pltpu.make_async_copy(
+            wd.at[:, pl.ds(n * kc, kc)], w_out.at[n % 2], out_sem.at[n % 2])
+
+    barrier = pltpu.get_barrier_semaphore()
+    for d in range(1, EXPERTS):
+        pl.semaphore_signal(barrier, inc=1, device_id={"tp": peer(d) * 2 + core}, device_id_type=MESH)
+    pl.semaphore_signal(barrier, inc=1, device_id=twin, device_id_type=MESH)
+    for c in range(PARTS):
+        for cp in in_copies(c):
+            cp.start()
+    for n in range(2):
+        out_copy(n).start()
+
+    lane = iota((n_tok, rows), 1)
+    lane_group = lane >> 4
+    place = lane & 15
+    first = routes[:, 0:1] == lane_group
+    second = routes[:, 1:2] == lane_group
+    named = jnp.where(first | second, 1.0, 0.0).astype(F32)
+    gate = jnp.where(first, gates[:, 0:1], 0.0) + jnp.where(second, gates[:, 1:2], 0.0)
+    earlier = jnp.where(iota((n_tok, n_tok), 1) < iota((n_tok, n_tok), 0), 1.0, 0.0).astype(BF)
+    slot = jnp.dot(earlier, named.astype(BF), preferred_element_type=F32).astype(jnp.int32)
+    main = jnp.where(slot == place, named, 0.0)
+    over = jnp.where(slot == BASE + (place >> 3), named, 0.0)
+    overs = jnp.concatenate(
+        [jnp.where((lane & 7) == k, over, 0.0) for k in range(8)], axis=0)
+    flipped = jnp.concatenate([overs, main, jnp.zeros_like(main)], axis=0).T.astype(BF)
+    over_t, main_t = flipped[:, :8 * n_tok], flipped[:, 8 * n_tok:9 * n_tok]
+    full = jnp.concatenate([overs * jnp.concatenate([gate] * 8, axis=0), main * gate], axis=0)
+    high = full.astype(BF)
+    gsc[0] = high
+    gsc[1] = (full - high.astype(F32)).astype(BF)
+
+    i, j = iota((rows, rows), 0), iota((rows, rows), 1)
+    unpack = ((i >> 4) == (j & 7)) & (((i & 15) >> 1) == (j >> 4)) & ((i & 1) == ((j & 15) >> 3))
+    unpack = jnp.where(unpack, 1.0, 0.0).astype(BF)
+    pack = ((j >> 4) == (i & 7)) & (((j & 15) >> 1) == (i >> 4)) & ((j & 1) == ((i & 15) >> 3))
+    pack = jnp.where(pack, 1.0, 0.0).astype(BF)
+
+    def block(g):
+        return pl.ds(pl.multiple_of(g * BASE, BASE), BASE)
+
+    def ship(src, dst, s_sem, r_sem, c, d):
+        to = peer(d)
+        return pltpu.make_async_remote_copy(
+            src_ref=src.at[c, block(to)], dst_ref=dst.at[c, block(group)],
+            send_sem=s_sem.at[c, d], recv_sem=r_sem.at[c, group],
+            device_id={"tp": to * 2 + core}, device_id_type=MESH)
+
+    def landed(dst, s_sem, r_sem, c, d):
+        src = lax.rem(group + EXPERTS - d, EXPERTS)
+        return pltpu.make_async_remote_copy(
+            src_ref=dst.at[c, block(src)], dst_ref=dst.at[c, block(src)],
+            send_sem=s_sem.at[c, d], recv_sem=r_sem.at[c, src],
+            device_id=twin, device_id_type=MESH)
+
+    for c in range(PARTS):
+        cols = tok[:, c * kc:(c + 1) * kc]
+        send[c, :, :kc] = jnp.dot(main_t, cols, preferred_element_type=F32).astype(BF)
+        tall = jnp.concatenate([cols[:, k * ow:(k + 1) * ow] for k in range(8)], axis=0)
+        send[c, :, kc:] = jnp.dot(over_t, tall, preferred_element_type=F32).astype(BF)
+        if c == 0:
+            pl.semaphore_wait(barrier, EXPERTS)
+        for d in range(1, EXPERTS):
+            ship(send, recv_a, ssem, rsem, c, d).start()
+        recv_a[c, block(group), :] = send[c, block(group), :]
+
+    def spread(src, c, at):
+        x[at:at + rows, :] = src[c, :, :kc]
+        wide = jnp.dot(unpack, src[c, :, kc:], preferred_element_type=F32).astype(BF)
+        for k in range(8):
+            x[at + rows:at + half, k * ow:(k + 1) * ow] = wide[k * ext:(k + 1) * ext]
+
+    def forward(c):
+        return pltpu.make_async_remote_copy(
+            src_ref=recv_a.at[c], dst_ref=recv_b.at[c], send_sem=fs_sem.at[c],
+            recv_sem=fr_sem.at[c], device_id=twin, device_id_type=MESH)
+
+    for c in range(PARTS):
+        for d in range(1, EXPERTS):
+            landed(recv_a, ssem, rsem, c, d).wait_recv()
+        forward(c).start()
+        spread(recv_a, c, 0)
+        for cp in in_copies(c):
+            cp.wait()
+        forward(c).wait_recv()
+        spread(recv_b, c, half)
+
+        def tile(t, carry):
+            cols = pl.ds(pl.multiple_of(t * 2 * tw, 128), 2 * tw)
+            both = jnp.dot(x[...], w_in[c, :, cols], preferred_element_type=F32)
+            if c > 0:
+                both = both + acc[:, cols]
+            if c < PARTS - 1:
+                acc[:, cols] = both
+            else:
+                g, u = both[:, :tw], both[:, tw:]
+                hid[:, pl.ds(pl.multiple_of(t * tw, 128), tw)] = (
+                    g / (1.0 + jnp.exp(-g)) * u).astype(BF)
+            return carry
+
+        lax.fori_loop(0, NT, tile, 0)
+
+    def swap(n):
+        return pltpu.make_async_remote_copy(
+            src_ref=part_s.at[n], dst_ref=part_r.at[n], send_sem=ps_sem.at[n],
+            recv_sem=pr_sem.at[n], device_id=twin, device_id_type=MESH)
+
+    def finish(n):
+        swap(n).wait_recv()
+        total = (own[n % 2] + part_r[n].astype(F32)).astype(BF)
+        rsend[n, :, :kc] = total[:rows]
+        tall = jnp.concatenate(
+            [total[rows:, k * ow:(k + 1) * ow] for k in range(8)], axis=0)
+        rsend[n, :, kc:] = jnp.dot(pack, tall, preferred_element_type=F32).astype(BF)
+        for d in range(1, EXPERTS):
+            ship(rsend, ret, bs_sem, br_sem, n, d).start()
+        ret[n, block(group), :] = rsend[n, block(group), :]
+
+    for n in range(PARTS):
+        out_copy(n).wait()
+
+        def down(t, carry):
+            cols = pl.ds(pl.multiple_of(t * 512, 512), 512)
+            res = jnp.dot(hid[...], w_out[n % 2, :, cols], preferred_element_type=F32)
+            own[n % 2, :, cols] = res[:half]
+            part_s[n, :, cols] = res[half:].astype(BF)
+            return carry
+
+        lax.fori_loop(0, kc // 512, down, 0)
+        swap(n).start()
+        if n == 0:
+            out_copy(2).start()
+        if n > 0:
+            finish(n - 1)
+    finish(PARTS - 1)
+
+    for n in range(PARTS):
+        for d in range(1, EXPERTS):
+            landed(ret, bs_sem, br_sem, n, d).wait_recv()
+        base, extra = ret[n, :, :kc], ret[n, :, kc:]
+        res = jnp.dot(gsc[0, 8 * n_tok:], base, preferred_element_type=F32)
+        res = res + jnp.dot(gsc[1, 8 * n_tok:], base, preferred_element_type=F32)
+        add = jnp.dot(gsc[0, :8 * n_tok], extra, preferred_element_type=F32)
+        add = add + jnp.dot(gsc[1, :8 * n_tok], extra, preferred_element_type=F32)
+        for k in range(8):
+            out[:, n * kc + k * ow:n * kc + (k + 1) * ow] = (
+                res[:, k * ow:(k + 1) * ow] + add[k * n_tok:(k + 1) * n_tok]).astype(BF)
+
+    for c in range(PARTS):
+        for d in range(1, EXPERTS):
+            ship(send, recv_a, ssem, rsem, c, d).wait_send()
+            ship(rsend, ret, bs_sem, br_sem, c, d).wait_send()
+        forward(c).wait_send()
+        swap(c).wait_send()
+
+
+def local_pair(tokens, routes, gates, w_gate, w_up, w_down):
+    n_tok, feat = tokens.shape
+    ff = w_gate.shape[1]
+    kc = feat // PARTS
+    mw = kc + kc // 8
+    rows = EXPERTS * BASE
+    half = rows + EXPERTS * 2
+    dma = pltpu.SemaphoreType.DMA
+    vmem = pl.BlockSpec(memory_space=pltpu.VMEM)
+    hbm = pl.BlockSpec(memory_space=pl.ANY)
+    return pl.pallas_call(
+        kernel,
+        out_shape=jax.ShapeDtypeStruct((n_tok, feat), BF),
+        in_specs=[vmem] * 3 + [hbm] * 3,
+        out_specs=vmem,
+        scratch_shapes=[
+            pltpu.VMEM((PARTS, kc, 2 * ff), BF),
+            pltpu.VMEM((2, ff, kc), BF),
+            pltpu.VMEM((2 * half, 2 * ff), F32),
+            pltpu.VMEM((2 * half, ff), BF),
+            pltpu.VMEM((2 * half, kc), BF),
+            pltpu.VMEM((PARTS, rows, mw), BF),
+            pltpu.VMEM((PARTS, rows, mw), BF),
+            pltpu.VMEM((PARTS, rows, mw), BF),
+            pltpu.VMEM((2, half, kc), F32),
+            pltpu.VMEM((PARTS, half, kc), BF),
+            pltpu.VMEM((PARTS, half, kc), BF),
+            pltpu.VMEM((PARTS, rows, mw), BF),
+            pltpu.VMEM((PARTS, rows, mw), BF),
+            pltpu.VMEM((2, 9 * n_tok, rows), BF),
+            dma((PARTS, 2 * NT)),
+            dma((2,)),
+            dma((PARTS, EXPERTS)),
+            dma((PARTS, EXPERTS)),
+            dma((PARTS,)),
+            dma((PARTS,)),
+            dma((PARTS,)),
+            dma((PARTS,)),
+            dma((PARTS, EXPERTS)),
+            dma((PARTS, EXPERTS)),
+        ],
+        compiler_params=pltpu.CompilerParams(
+            collective_id=0, has_side_effects=True, vmem_limit_bytes=62 * 2**20),
+    )(tokens, routes, gates, w_gate, w_up, w_down)
+
+
 def solution(mesh):
     in_specs = (
         P(("parts", "tp"), None),
@@ -78,4 +329,5 @@
         P("tp", None),
     )
     out_specs = P(("parts", "tp"), None)
+    local = local_pair if mesh.shape["tp"] == 2 * EXPERTS else local_any
     return jax.shard_map(local, mesh=mesh, in_specs=in_specs, out_specs=out_specs, check_vma=False)

time: 189 us -> 67.3 us (0.36)
  the two profiles are of different devices: /device:TPU:30 before, /device:TPU:0 now
where the time goes in v1:
time: 67.3 us; the launch traced here: 67 us
  Pallas kernels  62.5 us (93%)
  local copies, waits for them, and re-layouts  4.52 us (7%)
    pallas_call x1, Pallas kernels, local_pair(): pl.pallas_call(kernel, out_shape=jax.ShapeDtypeStruct((n_tok, feat), BF),...  62.5 us
    unnamed x3, local copies, waits for them, and re-layouts  4.52 us

profile of v1, /device:TPU:0, one launch (start us, length us, event | category | flops | bytes accessed | tf_op | source)
XLA Modules:
  0.0 67.0 jit_solution(3496823843715041944)
XLA Ops:
  0.0 1.4 %copy.7.routes = s32[64,2]{1,0:T(8,128)} copy(s32[64,2]{0,1:T(2,128)} %param.7) | data formatting | bytes 1024 | tf_op args[1]
  1.4 1.4 %copy.8.gates = f32[64,2]{1,0:T(8,128)} copy(f32[64,2]{0,1:T(2,128)} %param.8) | data formatting | bytes 1024 | tf_op args[2]
  2.7 62.5 %shard_map.64 = bf16[64,3072]{1,0:T(8,128)(2,1)} custom-call(bf16[64,3072]{1,0:T(8,128)(2,1)} %tok.1, s32[64,2]{1,0:T(8,128)} %copy.7.routes, f32[64,2]{1,0:T(8,128)} %copy.8.gates, bf16[3072,2688]{1,0:T(8,128)(2,1)} %wg.1, bf16[3072,2688]{1,0:T(8,128)(2,1)} %wu.1, bf16[2688,3072]{1,0:T(8,128)(2,1)} %wd.1), custom_call_target="tpu_custom_call" | custom-call | tf_op jit(solution)/shard_map/pallas_call | solution.py:286
  65.3 1.8 %copy.10 = bf16[64,3072]{1,0:T(8,128)(2,1)} copy(bf16[64,3072]{1,0:T(8,128)(2,1)} %shard_map.64) | data formatting | bytes 786432

commit v2 on v1

v2 whole, which is shorter than its diff:
```python
import functools

import jax
import jax.numpy as jnp
from jax import lax
from jax.experimental import pallas as pl
from jax.experimental.pallas import tpu as pltpu
from jax.sharding import PartitionSpec as P

EXPERTS = 8
TOP = 2
CAP = 18
BASE = 16
MESH = pl.DeviceIdType.MESH
BF = jnp.bfloat16
F32 = jnp.float32


def swapped(x, axis, bit):
    return lax.ppermute(x, axis, [(i, i ^ 1 << bit) for i in range(lax.axis_size(axis))])


def passed_along(value, axis, steps):
    count = lax.axis_size(axis)
    pairs = [(source, (source + steps) % count) for source in range(count)]
    return lax.ppermute(value, axis, pairs)


def expert_rows(chosen_rows, w_gate, w_up, w_down):
    gate_act = jnp.dot(chosen_rows, w_gate, preferred_element_type=jnp.float32)
    up_act = jnp.dot(chosen_rows, w_up, preferred_element_type=jnp.float32)
    hidden = (jax.nn.silu(gate_act) * up_act).astype(jnp.bfloat16)
    return jnp.dot(hidden, w_down, preferred_element_type=jnp.float32)


def local_any(tokens, routes, gates, w_gate, w_up, w_down):
    devices = lax.axis_size("tp")
    cycle_size = devices // EXPERTS
    levels = cycle_size.bit_length() - 1
    my_index = lax.axis_index("tp")
    my_group = my_index // cycle_size
    tok_count, feat_width = tokens.shape
    routed = routes.reshape(-1)
    pair_count = routed.shape[0]
    onehot = (routed[:, None] == jnp.arange(EXPERTS, dtype=jnp.int32)[None, :]).astype(jnp.int32)
    before = jnp.cumsum(onehot, axis=0) - onehot
    slot_index = jnp.sum(before * onehot, axis=1)
    target = routed * CAP + slot_index
    source_tok = jnp.arange(pair_count, dtype=jnp.int32) // TOP
    outgoing = (
        jnp.zeros((EXPERTS * CAP, feat_width), jnp.bfloat16).at[target].set(tokens[source_tok])
    )
    outgoing = outgoing.reshape(EXPERTS, CAP, feat_width)
    group_order = (my_group - jnp.arange(EXPERTS, dtype=jnp.int32)) % EXPERTS
    spread = jnp.repeat(outgoing, cycle_size, axis=0)
    incoming = lax.all_to_all(spread, "tp", split_axis=0, concat_axis=0, tiled=True)
    flat_rows = incoming.reshape(devices * CAP, feat_width)
    partial_value = expert_rows(flat_rows, w_gate, w_up, w_down)
    partial_value = partial_value.astype(jnp.bfloat16).reshape(devices, CAP, feat_width)
    current = lax.optimization_barrier(partial_value).astype(jnp.float32)
    current = current.reshape(EXPERTS, cycle_size, CAP, feat_width)
    for bit in range(levels):
        halves = current.reshape(EXPERTS, current.shape[1] // 2, 2, CAP, feat_width)
        upper = my_index // (1 << bit) % 2 == 1
        kept = jnp.where(upper, halves[:, :, 1], halves[:, :, 0])
        sending = jnp.where(upper, halves[:, :, 0], halves[:, :, 1])
        current = kept + swapped(sending.astype(jnp.bfloat16), "tp", bit).astype(sending.dtype)
    owned = current.reshape(EXPERTS, CAP, feat_width)
    back = [lax.dynamic_index_in_dim(owned, my_group, 0, keepdims=False)]
    for offset in range(1, EXPERTS):
        chosen = lax.dynamic_index_in_dim(owned, (my_group + offset) % EXPERTS, 0, keepdims=False)
        back.append(passed_along(chosen, "tp", offset * cycle_size))
    expert_out = jnp.take(jnp.stack(back), group_order, axis=0)
    picked = expert_out.reshape(EXPERTS * CAP, feat_width)[target]
    weighted = picked.reshape(tok_count, TOP, feat_width) * gates[:, :, None]
    return jnp.sum(weighted, axis=1).astype(jnp.bfloat16)


PARTS = 4
GROUPS = PARTS // 2
SLOTS = PARTS // 2 + 1
NT = 7


def iota(shape, dim):
    return lax.broadcasted_iota(jnp.int32, shape, dim)


def ones_where(mask, dtype=F32):
    return jnp.where(mask, 1.0, 0.0).astype(dtype)


def kernel(
    tok_hbm, routes, gates, wg, wu, wd, out,
    tok, w_in, w_out, acc, hid, x, send, recv_a, recv_b, own, part_s, part_r, wide, rsend, ret,
    gsc, res,
    tok_sem, in_sem, out_sem, ssem, rsem, fs_sem, fr_sem, ps_sem, pr_sem, bs_sem, br_sem,
):
    n_tok, feat = tok.shape
    kc = feat // PARTS
    ow = feat // 8
    ff = wg.shape[1]
    tw = ff // NT
    gr = feat // GROUPS
    rows = EXPERTS * BASE
    ext = EXPERTS * 2
    half = rows + ext
    me = lax.axis_index("tp")
    group = lax.div(me, 2)
    core = lax.rem(me, 2)
    twin = {"tp": group * 2 + (1 - core)}

    def peer(d):
        return lax.rem(group + d, EXPERTS)

    def in_copies(q):
        found = []
        for j in range(NT):
            for s, w in enumerate((wg, wu)):
                found.append(pltpu.make_async_copy(
                    w.at[pl.ds(q * gr, gr), pl.ds(j * tw, tw)],
                    w_in.at[pl.ds(q * gr, gr), pl.ds((2 * j + s) * tw, tw)],
                    in_sem.at[q, 2 * j + s]))
        return found

    def out_copy(n):
        return pltpu.make_async_copy(
            wd.at[:, pl.ds(n * kc, kc)], w_out.at[n % SLOTS], out_sem.at[n % SLOTS])

    def block(g):
        return pl.ds(pl.multiple_of(g * BASE, BASE), BASE)

    def there(c):
        return pl.ds(0, ow + kc) if c == 0 else pl.ds(ow + c * kc, kc)

    def home(n):
        return pl.ds(n * kc, kc + ow) if n == PARTS - 1 else pl.ds(n * kc, kc)

    barrier = pltpu.get_barrier_semaphore()
    for d in range(1, EXPERTS):
        pl.semaphore_signal(
            barrier, inc=1, device_id={"tp": peer(d) * 2 + core}, device_id_type=MESH)
    pl.semaphore_signal(barrier, inc=1, device_id=twin, device_id_type=MESH)
    fetch = pltpu.make_async_copy(tok_hbm, tok, tok_sem)
    fetch.start()

    def tiled(v):
        return jnp.concatenate([v] * 8, axis=1)

    line = iota((rows, n_tok), 0)
    named = ones_where((routes[0:1] == line >> 4) | (routes[1:2] == line >> 4), BF)
    wide_t = 8 * n_tok
    lane = iota((n_tok, wide_t), 1)
    earlier = ones_where(iota((n_tok, wide_t), 0) < lane & (n_tok - 1), BF)
    slot = jnp.dot(named, earlier, preferred_element_type=F32).astype(jnp.int32)
    line8 = iota((rows, wide_t), 0)
    lane8 = iota((rows, wide_t), 1)
    r8 = tiled(routes[...])
    first, second = r8[0:1] == line8 >> 4, r8[1:2] == line8 >> 4
    named8 = first | second
    over = named8 & (slot == BASE + ((line8 & 15) >> 3)) & (lane8 // n_tok == line8 & 7)
    main = named8 & (slot == line8 & 15)
    over_t = ones_where(over, BF)
    main_t = ones_where(main, BF)[:, :n_tok]

    def ship(src, dst, s_sem, r_sem, cols, c, d):
        to = peer(d)
        return pltpu.make_async_remote_copy(
            src_ref=src.at[block(to), cols], dst_ref=dst.at[block(group), cols],
            send_sem=s_sem.at[c, d], recv_sem=r_sem.at[c, group],
            device_id={"tp": to * 2 + core}, device_id_type=MESH)

    def landed(dst, s_sem, r_sem, cols, c, d):
        src = lax.rem(group + EXPERTS - d, EXPERTS)
        return pltpu.make_async_remote_copy(
            src_ref=dst.at[block(src), cols], dst_ref=dst.at[block(src), cols],
            send_sem=s_sem.at[c, d], recv_sem=r_sem.at[c, src],
            device_id=twin, device_id_type=MESH)

    def depart(c):
        for d in range(1, EXPERTS):
            ship(send, recv_a, ssem, rsem, there(c), c, d).start()

    fetch.wait()
    for c in range(PARTS):
        if c == 0:
            tall = jnp.concatenate([tok[:, k * ow:(k + 1) * ow] for k in range(8)], axis=0)
            send[:, :ow] = jnp.dot(over_t, tall, preferred_element_type=F32).astype(BF)
        send[:, ow + c * kc:ow + (c + 1) * kc] = jnp.dot(
            main_t, tok[:, c * kc:(c + 1) * kc], preferred_element_type=F32).astype(BF)
        if c == 0:
            pl.semaphore_wait(barrier, EXPERTS)
        if c < 2:
            depart(c)
        recv_a[block(group), there(c)] = send[block(group), there(c)]
        if c == 0:
            for cp in in_copies(0):
                cp.start()
    for q in range(1, GROUPS):
        for cp in in_copies(q):
            cp.start()
    for n in range(SLOTS):
        out_copy(n).start()

    g8 = tiled(gates[...])
    gate = jnp.where(first, g8[0:1], 0.0) + jnp.where(second, g8[1:2], 0.0)
    for at, size, full in (
        (0, wide_t, jnp.where(over, gate, 0.0)),
        (wide_t, n_tok, jnp.where(main, gate, 0.0)[:, :2 * n_tok]),
    ):
        full = full.T[:size]
        high = full.astype(BF)
        gsc[0, at:at + size] = high
        gsc[1, at:at + size] = (full - high.astype(F32)).astype(BF)

    i, j = iota((rows, rows), 0), iota((rows, rows), 1)
    unpack = ones_where(
        ((i >> 4) == (j & 7)) & (((i & 15) >> 1) == (j >> 4)) & ((i & 1) == ((j & 15) >> 3)), BF)
    pack = ones_where(
        ((j >> 4) == (i & 7)) & (((j & 15) >> 1) == (i >> 4)) & ((j & 1) == ((i & 15) >> 3)), BF)

    def spread(src, c, at):
        x[at:at + rows, c * kc:(c + 1) * kc] = src[:, ow + c * kc:ow + (c + 1) * kc]
        if c == 0:
            flat = jnp.dot(unpack, src[:, :ow], preferred_element_type=F32).astype(BF)
            for k in range(8):
                x[at + rows:at + half, k * ow:(k + 1) * ow] = flat[k * ext:(k + 1) * ext]

    def forward(c):
        return pltpu.make_async_remote_copy(
            src_ref=recv_a.at[:, there(c)], dst_ref=recv_b.at[:, there(c)],
            send_sem=fs_sem.at[c], recv_sem=fr_sem.at[c], device_id=twin, device_id_type=MESH)

    for c in range(PARTS):
        for d in range(1, EXPERTS):
            landed(recv_a, ssem, rsem, there(c), c, d).wait_recv()
        if c + 2 < PARTS:
            depart(c + 2)
        forward(c).start()
        spread(recv_a, c, 0)
        if c % (PARTS // GROUPS) == 0:
            for cp in in_copies(c // (PARTS // GROUPS)):
                cp.wait()
        forward(c).wait_recv()
        spread(recv_b, c, half)

        def tile(t, carry):
            cols = pl.ds(pl.multiple_of(t * 2 * tw, 128), 2 * tw)
            both = jnp.dot(
                x[:, c * kc:(c + 1) * kc], w_in[c * kc:(c + 1) * kc, cols],
                preferred_element_type=F32)
            if c > 0:
                both = both + acc[:, cols]
            if c < PARTS - 1:
                acc[:, cols] = both
            else:
                g, u = both[:, :tw], both[:, tw:]
                hid[:, pl.ds(pl.multiple_of(t * tw, 128), tw)] = (
                    g / (1.0 + jnp.exp(-g)) * u).astype(BF)
            return carry

        lax.fori_loop(0, NT, tile, 0)

    def swap(n):
        return pltpu.make_async_remote_copy(
            src_ref=part_s.at[n], dst_ref=part_r.at[n], send_sem=ps_sem.at[n],
            recv_sem=pr_sem.at[n], device_id=twin, device_id_type=MESH)

    def finish(n):
        swap(n).wait_recv()
        total = (own[n % 2] + part_r[n].astype(F32)).astype(BF)
        rsend[:, n * kc:(n + 1) * kc] = total[:rows]
        wide[:, n * kc:(n + 1) * kc] = total[rows:]
        if n == PARTS - 1:
            tall = jnp.concatenate([wide[:, k * ow:(k + 1) * ow] for k in range(8)], axis=0)
            rsend[:, feat:] = jnp.dot(pack, tall, preferred_element_type=F32).astype(BF)
        for d in range(1, EXPERTS):
            ship(rsend, ret, bs_sem, br_sem, home(n), n, d).start()
        ret[block(group), home(n)] = rsend[block(group), home(n)]

    for n in range(PARTS):
        out_copy(n).wait()
        down = jnp.dot(hid[...], w_out[n % SLOTS], preferred_element_type=F32)
        part_s[n] = down[half:].astype(BF)
        swap(n).start()
        own[n % 2] = down[:half]
        if n + SLOTS < PARTS:
            out_copy(n + SLOTS).start()
        if n > 0:
            finish(n - 1)
    finish(PARTS - 1)

    for n in range(PARTS):
        for d in range(1, EXPERTS):
            landed(ret, bs_sem, br_sem, home(n), n, d).wait_recv()
        base = ret[:, n * kc:(n + 1) * kc]
        here = jnp.dot(gsc[0, wide_t:], base, preferred_element_type=F32)
        res[:, n * kc:(n + 1) * kc] = here + jnp.dot(
            gsc[1, wide_t:], base, preferred_element_type=F32)
    extra = ret[:, feat:]
    add = jnp.dot(gsc[0, :wide_t], extra, preferred_element_type=F32)
    add = add + jnp.dot(gsc[1, :wide_t], extra, preferred_element_type=F32)
    for k in range(8):
        out[:, k * ow:(k + 1) * ow] = (
            res[:, k * ow:(k + 1) * ow] + add[k * n_tok:(k + 1) * n_tok]).astype(BF)

    for c in range(PARTS):
        for d in range(1, EXPERTS):
            ship(send, recv_a, ssem, rsem, there(c), c, d).wait_send()
            ship(rsend, ret, bs_sem, br_sem, home(c), c, d).wait_send()
        forward(c).wait_send()
        swap(c).wait_send()


def local_pair(tokens, routes, gates, w_gate, w_up, w_down):
    n_tok, feat = tokens.shape
    ff = w_gate.shape[1]
    kc = feat // PARTS
    mw = feat + feat // 8
    rows = EXPERTS * BASE
    half = rows + EXPERTS * 2
    dma = pltpu.SemaphoreType.DMA
    vmem = pl.BlockSpec(memory_space=pltpu.VMEM)
    hbm = pl.BlockSpec(memory_space=pl.ANY)
    return pl.pallas_call(
        kernel,
        out_shape=jax.ShapeDtypeStruct((n_tok, feat), BF),
        in_specs=[hbm] + [vmem] * 2 + [hbm] * 3,
        out_specs=vmem,
        scratch_shapes=[
            pltpu.VMEM((n_tok, feat), BF),
            pltpu.VMEM((feat, 2 * ff), BF),
            pltpu.VMEM((SLOTS, ff, kc), BF),
            pltpu.VMEM((2 * half, 2 * ff), F32),
            pltpu.VMEM((2 * half, ff), BF),
            pltpu.VMEM((2 * half, feat), BF),
            pltpu.VMEM((rows, mw), BF),
            pltpu.VMEM((rows, mw), BF),
            pltpu.VMEM((rows, mw), BF),
            pltpu.VMEM((2, half, kc), F32),
            pltpu.VMEM((PARTS, half, kc), BF),
            pltpu.VMEM((PARTS, half, kc), BF),
            pltpu.VMEM((EXPERTS * 2, feat), BF),
            pltpu.VMEM((rows, mw), BF),
            pltpu.VMEM((rows, mw), BF),
            pltpu.VMEM((2, 9 * n_tok, rows), BF),
            pltpu.VMEM((n_tok, feat), F32),
            dma,
            dma((GROUPS, 2 * NT)),
            dma((SLOTS,)),
            dma((PARTS, EXPERTS)),
            dma((PARTS, EXPERTS)),
            dma((PARTS,)),
            dma((PARTS,)),
            dma((PARTS,)),
            dma((PARTS,)),
            dma((PARTS, EXPERTS)),
            dma((PARTS, EXPERTS)),
        ],
        compiler_params=pltpu.CompilerParams(
            collective_id=0, has_side_effects=True, vmem_limit_bytes=63 * 2**20),
    )(tokens, routes.T, gates.T, w_gate, w_up, w_down)


def solution(mesh):
    in_specs = (
        P(("parts", "tp"), None),
        P(("parts", "tp"), None),
        P(("parts", "tp"), None),
        P(None, "tp"),
        P(None, "tp"),
        P("tp", None),
    )
    out_specs = P(("parts", "tp"), None)
    local = local_pair if mesh.shape["tp"] == 2 * EXPERTS else local_any
    return jax.shard_map(local, mesh=mesh, in_specs=in_specs, out_specs=out_specs, check_vma=False)
```

time: 67.3 us -> 63.5 us (0.944)
  local copies, waits for them, and re-layouts: 4.52 us -> 1.77 us
  Pallas kernels: 62.5 us -> 61.2 us
    unnamed x3 -> x1, local copies, waits for them, and re-layouts: 4.52 us -> 1.77 us
    pallas_call x1, Pallas kernels: 62.5 us -> 61.2 us  [local_pair(): pl.pallas_call(kernel, out_shape=jax.ShapeDtypeStruct((n_tok, feat), BF),...]
where the time goes in v2:
time: 63.5 us; the launch traced here: 63 us
  Pallas kernels  61.2 us (96%)
  local copies, waits for them, and re-layouts  1.77 us (3%)
    pallas_call x1, Pallas kernels, local_pair(): pl.pallas_call(kernel, out_shape=jax.ShapeDtypeStruct((n_tok, feat), BF),...  61.2 us
    unnamed x1, local copies, waits for them, and re-layouts  1.77 us

profile of v2, /device:TPU:0, one launch (start us, length us, event | category | flops | bytes accessed | tf_op | source)
XLA Modules:
  0.0 63.0 jit_solution(16545269007726997486)
XLA Ops:
  0.0 61.2 %shard_map.64 = bf16[64,3072]{1,0:T(8,128)(2,1)} custom-call(bf16[64,3072]{1,0:T(8,128)(2,1)} %tok_hbm.1, s32[2,64]{1,0:T(2,128)} %bitcast.2, f32[2,64]{1,0:T(2,128)} %bitcast.3, bf16[3072,2688]{1,0:T(8,128)(2,1)} %wg.1, bf16[3072,2688]{1,0:T(8,128)(2,1)} %wu.1, bf16[2688,3072]{1,0:T(8,128)(2,1)} %wd.1), custom_call_target="tpu_custom_call" | custom-call | tf_op jit(solution)/shard_map/pallas_call | solution.py:325
  61.3 1.8 %copy.8 = bf16[64,3072]{1,0:T(8,128)(2,1)} copy(bf16[64,3072]{1,0:T(8,128)(2,1)} %shard_map.64) | data formatting | bytes 786432

commit v3 on v2

--- a/solution.py
+++ b/solution.py
@@ -79,6 +79,7 @@
 PARTS = 4
 GROUPS = PARTS // 2
 SLOTS = PARTS // 2 + 1
+NEAR = (1, 7, 2, 6, 3, 5, 4)
 NT = 7
 
 
@@ -111,7 +112,7 @@
     twin = {"tp": group * 2 + (1 - core)}
 
     def peer(d):
-        return lax.rem(group + d, EXPERTS)
+        return lax.rem(group + NEAR[d - 1], EXPERTS)
 
     def in_copies(q):
         found = []
@@ -171,7 +172,7 @@
             device_id={"tp": to * 2 + core}, device_id_type=MESH)
 
     def landed(dst, s_sem, r_sem, cols, c, d):
-        src = lax.rem(group + EXPERTS - d, EXPERTS)
+        src = lax.rem(group + EXPERTS - NEAR[d - 1], EXPERTS)
         return pltpu.make_async_remote_copy(
             src_ref=dst.at[block(src), cols], dst_ref=dst.at[block(src), cols],
             send_sem=s_sem.at[c, d], recv_sem=r_sem.at[c, src],

time: 63.5 us -> 64.1 us (level)
  Pallas kernels: 61.2 us -> 62.1 us
    pallas_call x1, Pallas kernels: 61.2 us -> 62.1 us  [local_pair(): pl.pallas_call(kernel, out_shape=jax.ShapeDtypeStruct((n_tok, feat), BF),...]
where the time goes in v3:
time: 64.1 us; the launch traced here: 63.9 us
  Pallas kernels  62.1 us (97%)
  local copies, waits for them, and re-layouts  1.77 us (3%)
    pallas_call x1, Pallas kernels, local_pair(): pl.pallas_call(kernel, out_shape=jax.ShapeDtypeStruct((n_tok, feat), BF),...  62.1 us
    unnamed x1, local copies, waits for them, and re-layouts  1.77 us

profile of v3, /device:TPU:0, one launch (start us, length us, event | category | flops | bytes accessed | tf_op | source)
XLA Modules:
  0.0 63.9 jit_solution(14888228547805816431)
XLA Ops:
  0.0 62.1 %shard_map.64 = bf16[64,3072]{1,0:T(8,128)(2,1)} custom-call(bf16[64,3072]{1,0:T(8,128)(2,1)} %tok_hbm.1, s32[2,64]{1,0:T(2,128)} %bitcast.2, f32[2,64]{1,0:T(2,128)} %bitcast.3, bf16[3072,2688]{1,0:T(8,128)(2,1)} %wg.1, bf16[3072,2688]{1,0:T(8,128)(2,1)} %wu.1, bf16[2688,3072]{1,0:T(8,128)(2,1)} %wd.1), custom_call_target="tpu_custom_call" | custom-call | tf_op jit(solution)/shard_map/pallas_call | solution.py:326
  62.1 1.8 %copy.8 = bf16[64,3072]{1,0:T(8,128)(2,1)} copy(bf16[64,3072]{1,0:T(8,128)(2,1)} %shard_map.64) | data formatting | bytes 786432
